TPU v7x, 256 devices: a whole 4x4x8 slice. The times are simulated.
256 devices in a mesh: mem: 8 (over y, z_lo), gx: 8 (over x, core), gy: 4 (over z_hi).
Axes of the slice: x: 4, y: 4, z: 8 (z_hi: 4, z_lo: 2; z = z_hi * 2 + z_lo), core: 2. Of those that a mesh axis runs over, the one named last changes fastest.
Arguments:
- background_samples: float32 [256, 256, 1024], P('mem', 'gx', 'gy'), may hold values from -6 to 6
- measured_space_anomalies: float32 [256, 8, 4, 8192], P('mem', 'gx', 'gy'), may hold values from -32 to 32
- innovation_vector: float32 [8, 4, 8, 1024], P('gx', 'gy', 'mem'), may hold values from -6 to 6
- error_spread_squared: float32 [8, 4, 8, 1024], P('gx', 'gy', 'mem'), may hold values from 0.25 to 4
- measured_nearest_anchor: int32 [8, 4, 8, 1024], P('gx', 'gy', 'mem'), may hold values from 0 to 3
- active_measurement_tally: int32 [8, 4, 8], P('gx', 'gy', 'mem'), may hold values from 256 to 1024, as said below
Outputs:
- updated_sample_matrix: float32 [256, 256, 1024], P('mem', 'gx', 'gy')
Inputs may be any that keep to these rules, and one draw needn't show every extreme that they name: `active_measurement_tally`: some band has all 1024 slots live and some band only 256.
All inputs are finite; a program needn't handle non-finite values.
Results may differ from a plain program's by a relative error of at most 0.0003.
Values sent between devices are 32-bit elements; how exact they have to be, the bound alone decides.
A program may use at most 128 MiB of HBM per device.

v0:
```python
import jax
import jax.numpy as jnp
from jax import lax
from jax.sharding import PartitionSpec as P

CGX = 4
NS_STEPS = 12


precise = lax.Precision.HIGHEST


def split_up(array, dim, size):
    lengths = array.shape
    tiles = array.reshape(*lengths[:dim], size, lengths[dim] // size, *lengths[dim + 1 :])
    return jnp.moveaxis(tiles, dim, 0)


def piece_ends(length, count):
    turn = length // count
    if turn >= 8:
        turn -= turn % 8
    return [turn * k for k in range(1, count)]


def laid_out(tiles, dim):
    tiles = jnp.moveaxis(tiles, 0, dim)
    lengths = tiles.shape
    return tiles.reshape(*lengths[:dim], lengths[dim] * lengths[dim + 1], *lengths[dim + 2 :])


def cut_exchange(array, axis, pieces, split_dim, concat_dim):
    tiles = split_up(array, split_dim, lax.axis_size(axis))
    split_at = max(range(1, max(2, tiles.ndim - 1)), key=lambda d: tiles.shape[d])
    gathered = []
    for share in jnp.split(tiles, piece_ends(tiles.shape[split_at], pieces), axis=split_at):
        if share.size:
            gathered.append(lax.all_to_all(share, axis, split_axis=0, concat_axis=0, tiled=True))
    return laid_out(jnp.concatenate(gathered, axis=split_at), concat_dim)


def padded_2(block, sides, width):
    for axis, dim in sides:
        count = lax.axis_size(axis)
        forward = [(i, i + 1) for i in range(count - 1)]
        forward.append((count - 1, 0))
        backward = [(target, source) for source, target in forward]
        low = lax.ppermute(
            lax.slice_in_dim(block, block.shape[dim] - width, None, axis=dim), axis, forward
        )
        high = lax.ppermute(lax.slice_in_dim(block, 0, width, axis=dim), axis, backward)
        block = jnp.concatenate([low, block, high], axis=dim)
    return block


def passed_along(array, axis, by):
    size = lax.axis_size(axis)
    return lax.ppermute(array, axis, [(i, (i + by) % size) for i in range(size)])


def transforms_block(obs_block, departure, variance, assign, live_count):
    realization_indices = obs_block.shape[0]
    slots = obs_block.shape[1]
    live_mask = (jnp.arange(slots, dtype=jnp.int32) < live_count).astype(jnp.float32)
    points = jnp.arange(CGX, dtype=jnp.int32)
    distance = (assign[None, :] - points[:, None]).astype(jnp.float32)
    weights = jnp.exp(-0.5 * distance * distance) * live_mask[None, :] / variance[None, :]
    scaled = obs_block[None, :, :] * weights[:, None, :]
    identity = jnp.eye(realization_indices, dtype=jnp.float32)
    covariance = (
        jnp.einsum("pko,jo->pkj", scaled, obs_block, precision=precise)
        + (realization_indices - 1.0) * identity
    )
    right_side = jnp.einsum("pko,o->pk", scaled, departure, precision=precise)
    frob_norm = jnp.sqrt(jnp.sum(covariance * covariance, axis=(1, 2)))
    square_root = covariance / frob_norm[:, None, None]
    inverse = jnp.broadcast_to(identity, covariance.shape)
    for iteration in range(NS_STEPS):
        middle = 1.5 * identity - 0.5 * jnp.einsum(
            "pij,pjk->pik", inverse, square_root, precision=precise
        )
        square_root = jnp.einsum("pij,pjk->pik", square_root, middle, precision=precise)
        inverse = jnp.einsum("pij,pjk->pik", middle, inverse, precision=precise)
    posterior = (
        jnp.einsum("pij,pjk->pik", inverse, inverse, precision=precise) / frob_norm[:, None, None]
    )
    mean_weights = jnp.einsum("pkj,pj->pk", posterior, right_side, precision=precise)
    return (
        jnp.sqrt(realization_indices - 1.0) * inverse / jnp.sqrt(frob_norm)[:, None, None]
        + mean_weights[:, :, None]
    )


def tent_x(spacing):
    steps = jnp.arange(2 * spacing, dtype=jnp.float32)
    return 1.0 - jnp.abs(2.0 * steps + 1.0 - 2.0 * spacing) / (2.0 * spacing)


def tent_y(height):
    rows_here = jnp.arange(height, dtype=jnp.float32)
    middle = height // 2
    tent_below = jnp.where(
        rows_here < middle, (2.0 * middle - 2.0 * rows_here - 1.0) / (2.0 * height), 0.0
    )
    tent_above = jnp.where(
        rows_here >= middle, (2.0 * rows_here + 1.0 - 2.0 * middle) / (2.0 * height), 0.0
    )
    return (tent_below, 1.0 - tent_below - tent_above, tent_above)


def half_delta(segment, row_pair, tent_pair):
    realization_indices, width, height = segment.shape
    coarse = row_pair.shape[1]
    spacing = width // (coarse - 2)
    margin = 3 * spacing // 2
    padded = jnp.pad(segment, ((0, 0), (margin, margin), (0, 0)))
    cell_blocks = padded.reshape(realization_indices, coarse + 1, spacing, height)
    windows = jnp.concatenate([cell_blocks[:, :-1], cell_blocks[:, 1:]], axis=2)
    windows = windows.reshape(realization_indices, coarse, 2 * spacing * height)
    product = jnp.einsum("qckm,kcz->qcmz", row_pair, windows, precision=precise)
    product = product.reshape(2, coarse, realization_indices, 2 * spacing, height)
    weighted = jnp.sum(
        product * tent_x(spacing)[None, None, None, :, None] * tent_pair[:, None, None, None, :],
        axis=0,
    )
    front = jnp.pad(weighted[:, :, :spacing], ((0, 1), (0, 0), (0, 0), (0, 0)))
    behind = jnp.pad(weighted[:, :, spacing:], ((1, 0), (0, 0), (0, 0), (0, 0)))
    merged = (
        (front + behind)
        .transpose(1, 0, 2, 3)
        .reshape(realization_indices, (coarse + 1) * spacing, height)
    )
    return merged[:, margin : margin + width]


def per_device(
    background_samples,
    measured_space_anomalies,
    innovation_vector,
    error_spread_squared,
    measured_nearest_anchor,
    active_measurement_tally,
):
    gathered_obs = cut_exchange(measured_space_anomalies, "mem", 2, 3, 0)
    realization_indices = gathered_obs.shape[0]
    slots = innovation_vector.shape[3]
    obs_block = gathered_obs.reshape(realization_indices, slots)
    own_row = transforms_block(
        obs_block,
        innovation_vector.reshape(slots),
        error_spread_squared.reshape(slots),
        measured_nearest_anchor.reshape(slots),
        active_measurement_tally.reshape(()),
    )
    tile_cycle = padded_2(own_row[None], (("gx", 1), ("gy", 0)), 1)
    band_index = lax.axis_index("mem")
    band_count = lax.axis_size("mem")
    tile_y = lax.axis_index("gy")
    tiles_y = lax.axis_size("gy")
    row_below = passed_along(
        jnp.where(band_index == band_count - 1, tile_cycle[0], tile_cycle[1]), "mem", 1
    )
    row_above = passed_along(jnp.where(band_index == 0, tile_cycle[2], tile_cycle[1]), "mem", -1)
    row_below = jnp.where((tile_y == 0) & (band_index == 0), tile_cycle[1], row_below)
    row_above = jnp.where(
        (tile_y == tiles_y - 1) & (band_index == band_count - 1), tile_cycle[1], row_above
    )
    site_positions_array = lax.all_to_all(
        background_samples, "mem", split_axis=2, concat_axis=0, tiled=True
    )
    background_centroid = jnp.mean(site_positions_array, axis=0)
    sample_departure_matrix = site_positions_array - background_centroid[None]
    height = site_positions_array.shape[2]
    middle = height // 2
    tent_below, tent_own, tent_above = tent_y(height)
    bottom_portion = half_delta(
        sample_departure_matrix[:, :, :middle],
        jnp.stack([row_below, tile_cycle[1]]),
        jnp.stack([tent_below[:middle], tent_own[:middle]]),
    )
    top_portion = half_delta(
        sample_departure_matrix[:, :, middle:],
        jnp.stack([tile_cycle[1], row_above]),
        jnp.stack([tent_own[middle:], tent_above[middle:]]),
    )
    updated_sample_matrix = background_centroid[None] + jnp.concatenate(
        [bottom_portion, top_portion], axis=2
    )
    return lax.all_to_all(updated_sample_matrix, "mem", split_axis=0, concat_axis=2, tiled=True)


def solution(mesh):
    in_specs = (
        P("mem", "gx", "gy"),
        P("mem", "gx", "gy", None),
        P("gx", "gy", "mem", None),
        P("gx", "gy", "mem", None),
        P("gx", "gy", "mem", None),
        P("gx", "gy", "mem"),
    )
    out_specs = P("mem", "gx", "gy")
    return jax.shard_map(
        per_device, mesh=mesh, in_specs=in_specs, out_specs=out_specs, check_vma=False
    )
```

profile of v0, /device:TPU:66, one launch (start us, length us, event | category | flops | bytes accessed | tf_op | source)
XLA Modules:
  0.0 307.9 jit_solution(16242113466827087705)
XLA Ops:
  0.0 3.9 %reduce.3 = f32[32,8192]{1,0:T(8,128)S(1)} reduce(f32[32,1,1,8192]{3,2,1,0:T(1,128)} %param.7, f32[]{:T(128)} %constant.76), dimensions={1,2}, to_apply=%param.7.reduce_sub_computation | reduce | bytes 2097156 | tf_op args[1]
  5.7 6.0 %all-to-all-start.1 = ((f32[8,16,1,1,1024]{4,1,3,2,0:T(8,128)}), f32[8,16,1,1,1024]{4,1,3,2,0:T(8,128)S(1)}, u32[]{:S(2)}, u32[]{:S(2)}) async-start(f32[8,16,1,1,1024]{4,1,3,2,0:T(8,128)} %copy.28), calls=%async_computation.1 | async-start | bytes 1048576 | tf_op jit(solution)/shard_map/all_to_all | solution.py:38
  12.8 9.0 %all-to-all-done.1 = f32[8,16,1,1,1024]{4,1,3,2,0:T(8,128)S(1)} async-done(((f32[8,16,1,1,1024]{4,1,3,2,0:T(8,128)}), f32[8,16,1,1,1024]{4,1,3,2,0:T(8,128)S(1)}, u32[]{:S(2)}, u32[]{:S(2)}) %all-to-all-start.1) | async-done | bytes 524320 | tf_op jit(solution)/shard_map/all_to_all | solution.py:38
  21.7 3.5 %all-to-all-start.2 = ((f32[8,16,1,1,1024]{4,1,3,2,0:T(8,128)}), f32[8,16,1,1,1024]{4,1,3,2,0:T(8,128)S(1)}, u32[]{:S(2)}, u32[]{:S(2)}) async-start(f32[8,16,1,1,1024]{4,1,3,2,0:T(8,128)} %copy.29), calls=%async_computation.2 | async-start | bytes 1048576 | tf_op jit(solution)/shard_map/all_to_all | solution.py:38
  25.3 4.4 %copy.26 = f32[32,32,256]{1,0,2:T(8,128)} copy(f32[32,32,256]{2,1,0:T(8,128)S(1)} %copy-done.3) | data formatting | bytes 2097152 | tf_op args[0]
  29.7 4.9 %reshape.142 = f32[8,1,32768]{2,1,0:T(1,128)} reshape(f32[256,32,32]{2,1,0:T(8,128)} %bitcast.168) | data formatting | bytes 2097152
  36.2 6.1 %all-to-all-start = ((f32[8,1,32768]{2,1,0:T(1,128)}), f32[8,1,32768]{2,1,0:T(1,128)S(1)}, u32[]{:S(2)}, u32[]{:S(2)}) async-start(f32[8,1,32768]{2,1,0:T(1,128)} %reshape.142), calls=%async_computation | async-start | bytes 2097152 | tf_op jit(solution)/shard_map/all_to_all | solution.py:168
  43.1 5.1 %multiply_reduce_fusion = (f32[4]{0:T(128)S(1)}, f32[4,256,256]{2,1,0:T(8,128)S(1)}) fusion(f32[256,256]{1,0:T(8,128)S(1)} %fusion.38, f32[256,1024,1]{1,0,2:T(8,128)} %bitcast.181, f32[4,1024]{1,0:T(4,128)S(1)} %fusion.44, f32[256,1024]{1,0:T(8,128)} %bitcast.182), kind=kOutput, calls=%fused_computation.55 | convolution fusion | flops 3223060480 | bytes 3424272 | tf_op jit(solution)/shard_map/pko,jo->pkj/dot_general | solution.py:71
  48.3 1.2 fusion.34
  50.5 1.2 fusion.41
  51.7 1.2 fusion.33
  52.9 1.1 fusion.60
  54.0 1.1 fusion.61
  55.2 1.2 fusion.32
  56.4 1.3 fusion.62
  57.7 1.1 fusion.63
  58.8 1.2 fusion.31
  60.0 1.1 fusion.64
  61.2 1.1 fusion.65
  62.3 1.2 fusion.30
  63.5 1.1 fusion.66
  65.8 1.2 fusion.29
  67.0 1.1 fusion.68
  68.1 1.4 fusion.69
  69.5 1.2 fusion.28
  70.7 1.1 fusion.70
  73.0 1.2 fusion.27
  74.1 1.1 fusion.72
  76.4 1.2 fusion.26
  77.6 1.1 fusion.74
  79.9 1.6 fusion.25
  81.5 1.1 fusion.76
  82.7 1.1 fusion.77
  83.8 1.2 fusion.24
  85.0 1.1 fusion.78
  86.1 1.1 fusion.79
  87.3 1.2 fusion.23
  88.5 1.1 fusion.80
  89.6 1.1 convolution_divide_fusion
  90.8 3.9 %fusion = f32[1,4,256]{2,0,1:T(1,128)S(1)} fusion(f32[4,1024]{1,0:T(4,128)S(1)} %fusion.44, f32[256,1024]{1,0:T(8,128)S(1)} %bitcast.183, f32[1,1,1,1024]{3,2,1,0:T(1,128)S(1)} %copy-done), kind=kOutput, calls=%fused_computation | convolution fusion | flops 13631488 | bytes 1073152 | tf_op jit(solution)/shard_map/pko,o->pk/dot_general | solution.py:74
  96.5 3.4 %collective-permute-done.1 = f32[1,1,256,256]{3,2,1,0:T(8,128)S(1)} collective-permute-done((f32[1,1,256,256]{3,2,1,0:T(8,128)S(1)}, f32[1,1,256,256]{3,2,1,0:T(8,128)S(1)}, u32[]{:S(2)}, u32[]{:S(2)}) %collective-permute-start.1) | collective-permute-done | bytes 262176 | tf_op jit(solution)/shard_map/ppermute | solution.py:51
  99.9 1.9 collective-permute-done
  101.8 1.3 pad_maximum_fusion.2
  103.1 3.6 %collective-permute-start.2 = (f32[1,6,256,256]{3,2,1,0:T(8,128)}, f32[1,6,256,256]{3,2,1,0:T(8,128)}, u32[]{:S(2)}, u32[]{:S(2)}) collective-permute-start(f32[1,6,256,256]{3,2,1,0:T(8,128)} %pad_maximum_fusion.2), channel_id=1, source_target_pairs={{0,1},{1,2},{2,3},{3,0},{4,5},{5,6},{6,7},{7,4},{8,9},{9,10},{10,1... | collective-permute-start | bytes 4718600 | tf_op jit(solution)/shard_map/ppermute | solution.py:48
  108.8 4.4 %reduce.4 = f32[8,32768]{1,0:T(8,128)S(1)} reduce(f32[8,1,32768]{2,1,0:T(1,128)} %copy-done.2, f32[]{:T(128)} %broadcast.182), dimensions={1}, to_apply=%all_to_all.32.reduce_sub_computation | reduce | bytes 2097156 | tf_op jit(solution)/shard_map/all_to_all | solution.py:168
  113.2 3.3 %reshape.143 = f32[256,32,32]{2,1,0:T(8,128)} reshape(f32[8,32768]{1,0:T(8,128)S(1)} %reduce.4) | data formatting | bytes 2097152
  116.5 5.7 %copy.27 = f32[32,32,8,32]{0,2,3,1:T(8,128)} copy(f32[32,32,8,32]{1,0,3,2:T(8,128)} %bitcast.169) | data formatting | bytes 2097152 | tf_op jit(solution)/shard_map/all_to_all | solution.py:168
  122.2 3.3 %all_to_all.35 = f32[256,32,32]{0,2,1:T(8,128)S(1)} reshape(f32[8,32,32,32]{1,0,3,2:T(8,128)} %bitcast.167) | data formatting | bytes 2097152 | tf_op jit(solution)/shard_map/all_to_all | solution.py:168
  125.5 4.1 %bitcast_reduce_fusion = f32[32,32]{1,0:T(8,128)S(1)} fusion(f32[32,32,8,32]{0,2,3,1:T(8,128)} %copy.27), kind=kLoop, calls=%fused_computation.97 | loop fusion | flops 261120 | bytes 1052672 | tf_op jit(solution)/shard_map/reduce_sum | solution.py:171
  129.6 45.1 %collective-permute-done.2 = f32[1,6,256,256]{3,2,1,0:T(8,128)} collective-permute-done((f32[1,6,256,256]{3,2,1,0:T(8,128)}, f32[1,6,256,256]{3,2,1,0:T(8,128)}, u32[]{:S(2)}, u32[]{:S(2)}) %collective-permute-start.2) | collective-permute-done | bytes 1572896 | tf_op jit(solution)/shard_map/ppermute | solution.py:48
  174.6 4.6 %collective-permute-done.4 = f32[1,6,256,256]{3,2,1,0:T(8,128)} collective-permute-done((f32[1,6,256,256]{3,2,1,0:T(8,128)}, f32[1,6,256,256]{3,2,1,0:T(8,128)}, u32[]{:S(2)}, u32[]{:S(2)}) %collective-permute-start.4) | collective-permute-done | bytes 1572896 | tf_op jit(solution)/shard_map/ppermute | solution.py:51
  179.2 2.3 bitcast_select_fusion.1
  182.1 3.8 %collective-permute-start.5 = (f32[6,256,256]{2,1,0:T(8,128)S(1)}, f32[6,256,256]{2,1,0:T(8,128)S(1)}, u32[]{:S(2)}, u32[]{:S(2)}) collective-permute-start(f32[6,256,256]{2,1,0:T(8,128)S(1)} %get-tuple-element.12), channel_id=1, source_target_pairs={{0,224},{32,0},{64,32},{96,64},{128,96},{160,128},{192,160},{224,1... | collective-permute-start | bytes 4718600 | tf_op jit(solution)/shard_map/ppermute | solution.py:58
  187.1 34.1 %collective-permute-done.3 = f32[6,256,256]{2,1,0:T(8,128)S(1)} collective-permute-done((f32[6,256,256]{2,1,0:T(8,128)S(1)}, f32[6,256,256]{2,1,0:T(8,128)S(1)}, u32[]{:S(2)}, u32[]{:S(2)}) %collective-permute-start.3) | collective-permute-done | bytes 1572896 | tf_op jit(solution)/shard_map/ppermute | solution.py:58
  221.3 29.1 %collective-permute-done.5 = f32[6,256,256]{2,1,0:T(8,128)S(1)} collective-permute-done((f32[6,256,256]{2,1,0:T(8,128)S(1)}, f32[6,256,256]{2,1,0:T(8,128)S(1)}, u32[]{:S(2)}, u32[]{:S(2)}) %collective-permute-start.5) | collective-permute-done | bytes 1572896 | tf_op jit(solution)/shard_map/ppermute | solution.py:58
  251.5 3.1 %fusion.4 = f32[6,256,256]{1,2,0:T(8,128)S(1)} fusion(f32[256,6,256,1]{0,2,3,1:T(8,128)S(1)} %bitcast.174, f32[2,6,256,256]{3,2,1,0:T(8,128)S(1)} %get-tuple-element.8, f32[2,256]{1,0:T(2,128)S(1)} %mul.250, f32[256]{0:T(256)S(1)} %mul.238), kind=kOutput, calls=%fused_computation.7 | convolution fusion | flops 2417885184 | bytes 6294528 | tf_op jit(solution)/shard_map/qckm,kcz->qcmz/dot_general | solution.py:120
  255.0 3.1 %fusion.5 = f32[6,256,256]{1,2,0:T(8,128)S(1)} fusion(f32[256,6,256,1]{0,2,3,1:T(8,128)S(1)} %bitcast.173, f32[2,6,256,256]{3,2,1,0:T(8,128)S(1)} %get-tuple-element.7, f32[2,256]{1,0:T(2,128)S(1)} %mul.244, f32[256]{0:T(256)S(1)} %mul.238), kind=kOutput, calls=%fused_computation.9 | convolution fusion | flops 2417885184 | bytes 6294528 | tf_op jit(solution)/shard_map/qckm,kcz->qcmz/dot_general | solution.py:120
  258.7 4.4 %copy.32 = f32[256,32,32]{2,1,0:T(8,128)} copy(f32[256,32,32]{0,2,1:T(8,128)S(1)} %maximum_add_fusion) | data formatting | bytes 2097152 | tf_op jit(solution)/shard_map/add | solution.py:186
  263.1 3.9 %reshape.144 = f32[8,1,32768]{2,1,0:T(1,128)S(1)} reshape(f32[256,32,32]{2,1,0:T(8,128)} %copy.32) | data formatting | bytes 2097152
  267.0 21.8 %all_to_all.46 = f32[8,1,32768]{2,1,0:T(1,128)S(1)} all-to-all(f32[8,1,32768]{2,1,0:T(1,128)S(1)} %reshape.144), channel_id=1, replica_groups=mesh['mem'=8,'gx'=8,'gy'=4] {'mem'}, dimensions={0} | all-to-all | bytes 2097152 | tf_op jit(solution)/shard_map/all_to_all | solution.py:189
  288.8 3.2 %reduce.5 = f32[8,32768]{1,0:T(8,128)S(1)} reduce(f32[8,1,32768]{2,1,0:T(1,128)S(1)} %all_to_all.46, f32[]{:T(128)} %broadcast.182), dimensions={1}, to_apply=%all_to_all.38.reduce_sub_computation | reduce | bytes 2097156 | tf_op jit(solution)/shard_map/all_to_all | solution.py:189
  292.0 3.3 %reshape.145 = f32[256,32,32]{2,1,0:T(8,128)} reshape(f32[8,32768]{1,0:T(8,128)S(1)} %reduce.5) | data formatting | bytes 2097152
  295.3 8.0 %copy.34 = f32[32,32,8,32]{3,2,1,0:T(8,128)} copy(f32[32,32,8,32]{3,1,0,2:T(8,128)} %bitcast.170) | data formatting | bytes 2097152 | tf_op jit(solution)/shard_map/all_to_all | solution.py:189
  303.2 4.2 %all_to_all.41 = f32[32,32,256]{2,1,0:T(8,128)} reshape(f32[32,32,8,32]{3,2,1,0:T(8,128)} %copy.34) | data formatting | bytes 2097152 | tf_op jit(solution)/shard_map/all_to_all | solution.py:189
  (75 shorter events, 18.0 us)
Async XLA Ops:
  0.0 90.8 %copy-start = (f32[1,1,1,1024]{3,2,1,0:T(1,128)S(1)}, f32[1,1,1,1024]{3,2,1,0:T(1,128)}, u32[]{:S(2)}) copy-start(f32[1,1,1,1024]{3,2,1,0:T(1,128)} %param.8) | copy-start | bytes 12292
  5.7 19.5 %copy-start.3 = (f32[32,32,256]{2,1,0:T(8,128)S(1)}, f32[32,32,256]{2,1,0:T(8,128)}, u32[]{:S(2)}) copy-start(f32[32,32,256]{2,1,0:T(8,128)} %param.6) | copy-start | bytes 3145732
  5.7 16.0 %all-to-all-start.1 = ((f32[8,16,1,1,1024]{4,1,3,2,0:T(8,128)}), f32[8,16,1,1,1024]{4,1,3,2,0:T(8,128)S(1)}, u32[]{:S(2)}, u32[]{:S(2)}) async-start(f32[8,16,1,1,1024]{4,1,3,2,0:T(8,128)} %copy.28), calls=%async_computation.1 | async-start | bytes 1048576 | tf_op jit(solution)/shard_map/all_to_all | solution.py:38
  21.7 14.5 %all-to-all-start.2 = ((f32[8,16,1,1,1024]{4,1,3,2,0:T(8,128)}), f32[8,16,1,1,1024]{4,1,3,2,0:T(8,128)S(1)}, u32[]{:S(2)}, u32[]{:S(2)}) async-start(f32[8,16,1,1,1024]{4,1,3,2,0:T(8,128)} %copy.29), calls=%async_computation.2 | async-start | bytes 1048576 | tf_op jit(solution)/shard_map/all_to_all | solution.py:38
  29.6 5.6 %copy-start.5 = (f32[1,1,1,1024]{3,2,1,0:T(1,128)S(1)}, f32[1,1,1,1024]{3,2,1,0:T(1,128)}, u32[]{:S(2)}) copy-start(f32[1,1,1,1024]{3,2,1,0:T(1,128)} %param.9) | copy-start | bytes 12292
  29.6 5.6 %copy-start.6 = (s32[1,1,1,1024]{3,2,1,0:T(1,128)S(1)}, s32[1,1,1,1024]{3,2,1,0:T(1,128)}, u32[]{:S(2)}) copy-start(s32[1,1,1,1024]{3,2,1,0:T(1,128)} %param.10) | copy-start | bytes 12292
  36.2 71.1 %all-to-all-start = ((f32[8,1,32768]{2,1,0:T(1,128)}), f32[8,1,32768]{2,1,0:T(1,128)S(1)}, u32[]{:S(2)}, u32[]{:S(2)}) async-start(f32[8,1,32768]{2,1,0:T(1,128)} %reshape.142), calls=%async_computation | async-start | bytes 2097152 | tf_op jit(solution)/shard_map/all_to_all | solution.py:168
  89.6 1.2 copy-start.4
  96.0 3.9 %collective-permute-start.1 = (f32[1,1,256,256]{3,2,1,0:T(8,128)S(1)}, f32[1,1,256,256]{3,2,1,0:T(8,128)S(1)}, u32[]{:S(2)}, u32[]{:S(2)}) collective-permute-start(f32[1,1,256,256]{3,2,1,0:T(8,128)S(1)} %get-tuple-element.18), channel_id=1, source_target_pairs={{4,0},{8,4},{12,8},{16,12},{20,16},{24,20},{28,24},{0,28},{5,1},{9... | collective-permute-start | bytes 786440 | tf_op jit(solution)/shard_map/ppermute | solution.py:51
  96.0 5.8 %collective-permute-start = (f32[1,1,256,256]{3,2,1,0:T(8,128)S(1)}, f32[1,1,256,256]{3,2,1,0:T(8,128)S(1)}, u32[]{:S(2)}, u32[]{:S(2)}) collective-permute-start(f32[1,1,256,256]{3,2,1,0:T(8,128)S(1)} %get-tuple-element.17), channel_id=1, source_target_pairs={{0,4},{4,8},{8,12},{12,16},{16,20},{20,24},{24,28},{28,0},{1,5},{5... | collective-permute-start | bytes 786440 | tf_op jit(solution)/shard_map/ppermute | solution.py:48
  103.1 71.5 %collective-permute-start.2 = (f32[1,6,256,256]{3,2,1,0:T(8,128)}, f32[1,6,256,256]{3,2,1,0:T(8,128)}, u32[]{:S(2)}, u32[]{:S(2)}) collective-permute-start(f32[1,6,256,256]{3,2,1,0:T(8,128)} %pad_maximum_fusion.2), channel_id=1, source_target_pairs={{0,1},{1,2},{2,3},{3,0},{4,5},{5,6},{6,7},{7,4},{8,9},{9,10},{10,1... | collective-permute-start | bytes 4718600 | tf_op jit(solution)/shard_map/ppermute | solution.py:48
  106.7 72.5 %collective-permute-start.4 = (f32[1,6,256,256]{3,2,1,0:T(8,128)}, f32[1,6,256,256]{3,2,1,0:T(8,128)}, u32[]{:S(2)}, u32[]{:S(2)}) collective-permute-start(f32[1,6,256,256]{3,2,1,0:T(8,128)} %pad_maximum_fusion.2), channel_id=1, source_target_pairs={{1,0},{2,1},{3,2},{0,3},{5,4},{6,5},{7,6},{4,7},{9,8},{10,9},{11,1... | collective-permute-start | bytes 4718600 | tf_op jit(solution)/shard_map/ppermute | solution.py:51
  107.3 1.0 copy-start.2
  181.5 39.7 %collective-permute-start.3 = (f32[6,256,256]{2,1,0:T(8,128)S(1)}, f32[6,256,256]{2,1,0:T(8,128)S(1)}, u32[]{:S(2)}, u32[]{:S(2)}) collective-permute-start(f32[6,256,256]{2,1,0:T(8,128)S(1)} %get-tuple-element.11), channel_id=1, source_target_pairs={{0,32},{32,64},{64,96},{96,128},{128,160},{160,192},{192,224},{224... | collective-permute-start | bytes 4718600 | tf_op jit(solution)/shard_map/ppermute | solution.py:58
  182.1 68.3 %collective-permute-start.5 = (f32[6,256,256]{2,1,0:T(8,128)S(1)}, f32[6,256,256]{2,1,0:T(8,128)S(1)}, u32[]{:S(2)}, u32[]{:S(2)}) collective-permute-start(f32[6,256,256]{2,1,0:T(8,128)S(1)} %get-tuple-element.12), channel_id=1, source_target_pairs={{0,224},{32,0},{64,32},{96,64},{128,96},{160,128},{192,160},{224,1... | collective-permute-start | bytes 4718600 | tf_op jit(solution)/shard_map/ppermute | solution.py:58
  295.3 12.1 %copy-start.1 = (f32[1,1,1,1024]{3,2,1,0:T(1,128)S(1)}, f32[1,1,1,1024]{3,2,1,0:T(1,128)}, u32[]{:S(2)}) copy-start(f32[1,1,1,1024]{3,2,1,0:T(1,128)} %param.8) | copy-start | bytes 12292
where the time goes:
time: 313 us; the launch traced here: 308 us
  waiting for transfers between devices  127 us (41%)
  matrix products  58.4 us (19%)
  local copies, waits for them, and re-layouts  53.2 us (17%)
  starting transfers between devices  24 us (8%)
  blocking collectives  21.8 us (7%)
  other arithmetic  21.5 us (7%)
    ppermute x2, waiting for transfers between devices, passed_along(): lax.ppermute(array, axis, [(i, (i + by) % size) for i in range(size)])  63.3 us
    ppermute x2, waiting for transfers between devices, padded_2(): lax.ppermute(lax.slice_in_dim(block, block.shape[dim] - width, None, axis...  47 us
    unnamed x21, local copies, waits for them, and re-layouts  22.4 us
    all_to_all x1, blocking collectives, per_device(): lax.all_to_all(updated_sample_matrix, 'mem', split_axis=0, concat_axis=2,...  21.8 us
    dot_general x12, matrix products, transforms_block(): jnp.einsum('pij,pjk->pik', inverse, square_root, precision=precise)  14.4 us
    dot_general x12, matrix products, transforms_block(): inverse = jnp.einsum('pij,pjk->pik', middle, inverse, precision=precise)  13.8 us
    dot_general x11, matrix products, transforms_block(): jnp.einsum('pij,pjk->pik', square_root, middle, precision=precise)  12.8 us
    all_to_all x2, local copies, waits for them, and re-layouts, per_device(): lax.all_to_all(updated_sample_matrix, 'mem', split_axis=0, concat_axis=2,...  12.1 us
  transfers between devices with their start and end apart: 9, of which 7 were waited for; matrix products, arithmetic and copies ran while one was open for 28% of the time, Pallas kernels for 0%

commit v1 on v0

v1 whole, which is shorter than its diff:
```python
import math

import jax
import jax.numpy as jnp
from jax import lax
from jax.experimental import pallas as pl
from jax.experimental.pallas import tpu as pltpu
from jax.sharding import PartitionSpec as P

NS_PASSES = (3, 3, 3, 3, 2, 2)
MESH = pl.DeviceIdType.MESH
f32 = jnp.float32
bf16 = jnp.bfloat16
K = 256
NB = 8
MB = K // NB
SLOTS = 1024
CHUNKS = 4
CW = SLOTS // CHUNKS
LN = 128


def split(a, n):
    parts = []
    for i in range(n):
        part = a.astype(bf16)
        parts.append(part)
        if i < n - 1:
            a = a - part.astype(f32)
    return parts


def dot(a, b):
    return jnp.dot(a, b, preferred_element_type=f32)


def product(a, b):
    n = len(a)
    total = None
    for order in range(n - 1, -1, -1):
        for i in range(order, -1, -1):
            term = dot(a[i], b[order - i])
            total = term if total is None else total + term
    return total


def block_transpose(v):
    lane_block = lax.broadcasted_iota(jnp.int32, v[0].shape, 1) // 16
    for bit in (4, 2, 1):
        upper = (lane_block & bit) != 0
        new = list(v)
        for i in range(8):
            if i & bit == 0:
                a, b = v[i], v[i | bit]
                new[i] = jnp.where(upper, pltpu.roll(b, 16 * bit, 1), a)
                new[i | bit] = jnp.where(upper, b, pltpu.roll(a, LN - 16 * bit, 1))
        v = new
    return v


def column_of(g, xx):
    return (8 * g + 4 + xx) % 32


def kernel(
    bg, obs, dep, var, anchor, tally,
    out,
    bgs, outs, pk, yb, wts, cov, rhs, norm, y0, y1, y2, y3, z0, z1, z2, z3,
    pb, bh, bl, bh3, bl3, means, ts, tl, tr, cb, rb,
    bg_in, obs_send, obs_recv, bg_send, bg_recv, t_send, t_recv, c_send, c_recv,
):
    me = lax.axis_index("mem")
    gx = lax.axis_index("gx")
    gy = lax.axis_index("gy")
    gx_left, gx_right = lax.rem(gx + 7, 8), lax.rem(gx + 1, 8)
    gy_prev, gy_next = lax.rem(gy + 3, 4), lax.rem(gy + 1, 4)
    ys = (y0, y1, y2, y3)
    zs = (z0, z1, z2, z3)

    halves = [slice(0, LN), slice(LN, 2 * LN)]
    loads = [pltpu.make_async_copy(bg.at[:, halves[h]], bgs.at[h], bg_in.at[h]) for h in range(2)]
    for load in loads:
        load.start()

    barrier = pltpu.get_barrier_semaphore()

    def greet(**where):
        pl.semaphore_signal(barrier, inc=1, device_id=where, device_id_type=MESH)

    def each_peer(fn):
        def step(off, carry):
            fn(lax.rem(me + off, NB))
            return carry

        lax.fori_loop(1, NB, step, 0)

    def each_member(fn):
        def step(j, carry):
            fn(j)
            return carry

        lax.fori_loop(0, NB, step, 0)

    each_peer(lambda j: greet(mem=j))
    greet(gx=gx_left)
    greet(gx=gx_right)
    greet(mem=jnp.int32(0), gy=gy_next)
    greet(mem=jnp.int32(NB - 1), gy=gy_prev)

    @pl.when(me == 0)
    def _():
        each_member(lambda j: greet(mem=j, gy=gy_prev))

    @pl.when(me == NB - 1)
    def _():
        each_member(lambda j: greet(mem=j, gy=gy_next))

    mine = pl.ds(pl.multiple_of(me * MB, MB), MB)

    live = (lax.broadcasted_iota(jnp.int32, (1, SLOTS), 1) < tally[...]).astype(f32)
    for p in range(4):
        away = (anchor[...] - p).astype(f32)
        weight = jnp.exp(-0.5 * away * away) * live / var[...]
        wts[p : p + 1, :] = weight
        wts[p + 4 : p + 5, :] = weight * dep[...]

    pl.semaphore_wait(barrier, 11 + jnp.where((me == 0) | (me == NB - 1), NB, 0))

    def obs_copy(c, j):
        first = pl.multiple_of(j * SLOTS + c * CW, CW)
        return pltpu.make_async_remote_copy(
            src_ref=obs.at[:, pl.ds(first, CW)],
            dst_ref=yb.at[mine, pl.ds(c * CW, CW)],
            send_sem=obs_send,
            recv_sem=obs_recv.at[c],
            device_id={"mem": j},
            device_id_type=MESH,
        )

    for c in range(CHUNKS):
        first = pl.multiple_of(me * SLOTS + c * CW, CW)
        pltpu.make_async_copy(
            obs.at[:, pl.ds(first, CW)], yb.at[mine, pl.ds(c * CW, CW)], obs_recv.at[c]
        ).start()
        each_peer(lambda j: obs_copy(c, j).start())

    for load in loads:
        load.wait()
    for g in range(4):
        for half in range(2):
            v = [bgs[half, pl.ds(column_of(g, xx), MB, stride=32), :] for xx in range(8)]
            for i, w in enumerate(block_transpose(v)):
                pk[half * 8 + i, g] = w

    cov[...] = jnp.zeros_like(cov)
    rhs[...] = jnp.zeros_like(rhs)

    def cov_step(c, carry):
        lanes = pl.ds(pl.multiple_of(c * CW, CW), CW)
        here = yb.at[:, lanes]
        pltpu.make_async_copy(here, here, obs_recv.at[c]).wait()
        y = yb[:, lanes]
        yt = split(y.T, 3)
        for p in range(4):
            cov[p] += product(split(y * wts[p : p + 1, lanes], 3), yt)
        rhs[...] += product(split(wts[:, lanes], 3), yt)
        return carry

    lax.fori_loop(0, CHUNKS - 1, cov_step, 0)

    def bg_copies(b):
        def copy(src, dst, where):
            return pltpu.make_async_remote_copy(
                src_ref=src, dst_ref=dst, send_sem=bg_send, recv_sem=bg_recv,
                device_id=where, device_id_type=MESH,
            )

        to_next = lax.rem(gy + jnp.where(b == 0, 1, 0), 4)
        to_prev = lax.rem(gy + jnp.where(b == NB - 1, 3, 0), 4)
        below, above = lax.rem(2 * b + 15, 16), lax.rem(2 * b + 2, 16)
        return (
            lambda: copy(pk.at[pl.ds(2 * b, 2)], pb.at[pl.ds(1, 2), :, mine, :], {"mem": b}),
            lambda: copy(pk.at[below], pb.at[0, :, mine, :], {"mem": b, "gy": to_next}),
            lambda: copy(pk.at[above], pb.at[3, :, mine, :], {"mem": b, "gy": to_prev}),
        )

    def start_bg(b):
        for copy in bg_copies(b):
            copy().start()

    each_peer(start_bg)
    pltpu.make_async_copy(pk.at[pl.ds(2 * me, 2)], pb.at[pl.ds(1, 2), :, mine, :], bg_recv).start()
    for s, edge, which in ((0, 0, 1), (3, NB - 1, 2)):

        @pl.when(me == edge)
        def _():
            bg_copies(me)[which]().start()

        @pl.when(me != edge)
        def _():
            u = lax.rem(2 * me + (15 if s == 0 else 2), 16)
            pltpu.make_async_copy(pk.at[u], pb.at[s, :, mine, :], bg_recv).start()

    cov_step(jnp.int32(CHUNKS - 1), 0)

    row_id = lax.broadcasted_iota(jnp.int32, (K, K), 0)
    eye = (row_id == lax.broadcasted_iota(jnp.int32, (K, K), 1)).astype(f32)
    points = range(4)

    def two_steps(x, n):
        xs = [split(a, n) for a in x]
        xx = [product(a, a) for a in xs]
        us = [split(1.5 * x[p] - 0.5 * xx[p], n) for p in points]
        ms = [split(2.25 * eye - 1.5 * x[p] + 0.25 * xx[p], n) for p in points]
        v = [product(us[p], ms[p]) for p in points]
        return [2.25 * eye - 0.75 * x[p] - 0.5 * v[p] for p in points]

    def pair(n, last):
        zp = [split(z[...], n) for z in zs]
        yp = [split(y[...], n) for y in ys]
        w = two_steps([product(zp[p], yp[p]) for p in points], n)
        wp = [split(a, n) for a in w]
        for p in points:
            if not last:
                ys[p][...] = product(yp[p], wp[p])
            zs[p][...] = product(wp[p], zp[p])

    scaled = []
    for p in points:
        full = cov[p] + (K - 1.0) * eye
        size = jnp.sqrt(jnp.sum(full * full, axis=(0, 1), keepdims=True))
        norm[p : p + 1, :] = jnp.broadcast_to(size, (1, LN))
        scaled.append(full * (1.0 / size))
    w = two_steps(scaled, NS_PASSES[0])
    for p in points:
        ys[p][...] = product(split(scaled[p], NS_PASSES[0]), split(w[p], NS_PASSES[0]))
        zs[p][...] = w[p]
    exact = sum(1 for n in NS_PASSES[1:] if n == 3)
    lax.fori_loop(0, exact, lambda i, carry: (pair(3, False), carry)[1], 0)
    for k in range(1 + exact, 6):
        pair(NS_PASSES[k], k == 5)

    def finish(p):
        z = zs[p][...]
        size = norm[p : p + 1, 0:1]
        first = jnp.sum(z * rhs[p + 4 : p + 5, :], axis=1, keepdims=True)
        mean_weights = jnp.sum(z * first, axis=0, keepdims=True) / size
        ts[p] = z * (math.sqrt(K - 1.0) / jnp.sqrt(size)) + mean_weights

    def t_copy(p, dst, where, i):
        return pltpu.make_async_remote_copy(
            src_ref=ts.at[p], dst_ref=dst, send_sem=t_send.at[i], recv_sem=t_recv.at[i],
            device_id={"gx": where}, device_id_type=MESH,
        )

    to_left = t_copy(0, tr, gx_left, 0)
    to_right = t_copy(3, tl, gx_right, 1)
    finish(0)
    to_left.start()
    finish(3)
    to_right.start()
    finish(1)
    finish(2)

    pltpu.make_async_copy(pb, pb, bg_recv).wait()
    lane = lax.broadcasted_iota(jnp.int32, (1, LN), 1)
    xx = lane // 16
    weight_right = (xx.astype(f32) + 0.5) / 8.0
    weight_left = 1.0 - weight_right
    south_end = (me == 0) & (gy == 0)
    north_end = (me == NB - 1) & (gy == 3)
    for s in range(4):
        tent = 1.0 - jnp.abs((lane % 16).astype(f32) + (16 * s + 0.5 - 32.0)) / 32.0
        end = south_end if s < 2 else north_end
        tent = jnp.where(end, 0.0 if s in (0, 3) else 1.0, tent)
        cols = slice(s * LN, (s + 1) * LN)
        for g in range(4):
            slab = pb[s, g]
            mean = jnp.sum(slab, axis=0, keepdims=True) * (1.0 / K)
            means[4 * s + g : 4 * s + g + 1, :] = mean
            slab = slab - mean
            left, right = slab * (tent * weight_left), slab * (tent * weight_right)
            if g < 3:
                for i, part in enumerate((left, right)):
                    hi, lo = split(part, 2)
                    bh[g, i * K : (i + 1) * K, cols] = hi
                    bl[g, i * K : (i + 1) * K, cols] = lo
            else:
                east = xx < 4
                for i, part in enumerate((left, right)):
                    for k, kept in enumerate((east, jnp.logical_not(east))):
                        hi, lo = split(jnp.where(kept, part, 0.0), 2)
                        rows = slice((2 * k + i) * K, (2 * k + i + 1) * K)
                        bh3[rows, cols] = hi
                        bl3[rows, cols] = lo

    odd = lax.rem(me, 2)
    below, above = lax.rem(2 * me + 15, 16), lax.rem(2 * me + 2, 16)
    gy_below = lax.rem(gy + jnp.where(me == 0, 3, 0), 4)
    gy_above = lax.rem(gy + jnp.where(me == NB - 1, 1, 0), 4)

    def c_copies(g, j):
        rows = pl.ds(pl.multiple_of(j * MB, MB), MB)

        def copy(src, dst, where):
            return pltpu.make_async_remote_copy(
                src_ref=src, dst_ref=dst, send_sem=c_send, recv_sem=c_recv.at[g],
                device_id=where, device_id_type=MESH,
            )

        return (
            lambda: copy(cb.at[g, pl.ds(1, 2), rows, :], rb.at[g, odd, pl.ds(2 * me, 2)], {"mem": j}),
            lambda: copy(cb.at[g, 0, rows, :], rb.at[g, odd, below], {"mem": j, "gy": gy_below}),
            lambda: copy(cb.at[g, 3, rows, :], rb.at[g, odd, above], {"mem": j, "gy": gy_above}),
        )

    def start_c(g):
        def start(j):
            for copy in c_copies(g, j):
                copy().start()

        each_peer(start)
        pltpu.make_async_copy(
            cb.at[g, pl.ds(1, 2), mine, :], rb.at[g, odd, pl.ds(2 * me, 2)], c_recv.at[g]
        ).start()
        for s, edge, which, u in ((0, 0, 1, below), (3, NB - 1, 2, above)):

            @pl.when(me == edge)
            def _():
                c_copies(g, me)[which]().start()

            @pl.when(me != edge)
            def _():
                pltpu.make_async_copy(
                    cb.at[g, s, mine, :], rb.at[g, odd, u], c_recv.at[g]
                ).start()

    def shares(g, lhs, hi_ref, lo_ref):
        parts = [split(a, 2) for a in lhs]
        hi = jnp.concatenate([a[0] for a in parts], axis=1)
        lo = jnp.concatenate([a[1] for a in parts], axis=1)
        for pairs in range(2):
            cols = slice(2 * pairs * LN, 2 * (pairs + 1) * LN)
            b_hi, b_lo = hi_ref[:, cols], lo_ref[:, cols]
            total = (dot(lo, b_hi) + dot(hi, b_lo)) + dot(hi, b_hi)
            for i in range(2):
                s = 2 * pairs + i
                part = total[:, i * LN : (i + 1) * LN]
                if s in (1, 2):
                    part = part + means[4 * s + g : 4 * s + g + 1, :]
                cb[g, s] = part

    for g in range(3):
        shares(g, [ts[g], ts[g + 1]], bh.at[g], bl.at[g])
        start_c(g)
    to_left.wait_recv()
    to_right.wait_recv()
    shares(3, [ts[3], tr[...], tl[...], ts[0]], bh3, bl3)
    start_c(3)

    for g in range(4):
        pltpu.make_async_copy(rb.at[g], rb.at[g], c_recv.at[g]).wait()
        for half in range(2):
            v = [rb[g, 0, half * 8 + i] + rb[g, 1, half * 8 + i] for i in range(8)]
            for xx_, w in enumerate(block_transpose(v)):
                outs[half, pl.ds(column_of(g, xx_), MB, stride=32), :] = w
    stores = [pltpu.make_async_copy(outs.at[h], out.at[:, halves[h]], bg_in.at[h]) for h in range(2)]
    for store in stores:
        store.start()

    for store in stores:
        store.wait()

    to_left.wait_send()
    to_right.wait_send()
    most = yb.at[pl.ds(0, K - MB), :]
    pltpu.make_async_copy(most, most, obs_send).wait()
    most = pb.at[:, :, pl.ds(0, K - MB), :]
    pltpu.make_async_copy(most, most, bg_send).wait()
    most = cb.at[:, :, pl.ds(0, K - MB), :]
    pltpu.make_async_copy(most, most, c_send).wait()

    @pl.when((me == 0) | (me == NB - 1))
    def _():
        one = pb.at[0, :, pl.ds(0, MB), :]
        pltpu.make_async_copy(one, one, bg_send).wait()
        one = cb.at[:, 0, pl.ds(0, MB), :]
        pltpu.make_async_copy(one, one, c_send).wait()


def per_device(bg, obs, dep, var, anchor, tally):
    vmem = pl.BlockSpec(memory_space=pltpu.VMEM)
    anywhere = pl.BlockSpec(memory_space=pl.ANY)
    square = pltpu.VMEM((K, K), f32)
    dma = pltpu.SemaphoreType.DMA
    out = pl.pallas_call(
        kernel,
        out_shape=jax.ShapeDtypeStruct((MB * 32, 256), f32),
        in_specs=[anywhere, anywhere, vmem, vmem, vmem, vmem],
        out_specs=anywhere,
        scratch_shapes=[
            pltpu.VMEM((2, MB * 32, LN), f32),
            pltpu.VMEM((2, MB * 32, LN), f32),
            pltpu.VMEM((16, 4, MB, LN), f32),
            pltpu.VMEM((K, SLOTS), f32),
            pltpu.VMEM((8, SLOTS), f32),
            pltpu.VMEM((4, K, K), f32),
            pltpu.VMEM((8, K), f32),
            pltpu.VMEM((8, LN), f32),
            *[square] * 8,
            pltpu.VMEM((4, 4, K, LN), f32),
            pltpu.VMEM((3, 2 * K, 4 * LN), bf16),
            pltpu.VMEM((3, 2 * K, 4 * LN), bf16),
            pltpu.VMEM((4 * K, 4 * LN), bf16),
            pltpu.VMEM((4 * K, 4 * LN), bf16),
            pltpu.VMEM((16, LN), f32),
            pltpu.VMEM((4, K, K), f32),
            square,
            square,
            pltpu.VMEM((4, 4, K, LN), f32),
            pltpu.VMEM((4, 2, 16, MB, LN), f32),
            dma((2,)),
            dma,
            dma((CHUNKS,)),
            dma,
            dma,
            dma((2,)),
            dma((2,)),
            dma,
            dma((4,)),
        ],
        compiler_params=pltpu.CompilerParams(
            collective_id=0, has_side_effects=True, vmem_limit_bytes=48 << 20
        ),
        name="analysis",
    )(
        bg.reshape(MB * 32, 256),
        obs.reshape(MB, NB * SLOTS),
        dep.reshape(1, SLOTS),
        var.reshape(1, SLOTS),
        anchor.reshape(1, SLOTS),
        tally.reshape(1, 1),
    )
    return out.reshape(MB, 32, 256)


def solution(mesh):
    in_specs = (
        P("mem", "gx", "gy"),
        P("mem", "gx", "gy", None),
        P("gx", "gy", "mem", None),
        P("gx", "gy", "mem", None),
        P("gx", "gy", "mem", None),
        P("gx", "gy", "mem"),
    )
    return jax.shard_map(
        per_device, mesh=mesh, in_specs=in_specs, out_specs=P("mem", "gx", "gy"), check_vma=False
    )
```

time: 313 us -> 80.3 us (0.26)
  the two profiles are of different devices: /device:TPU:66 before, /device:TPU:2 now
where the time goes in v1:
time: 80.3 us; the launch traced here: 79.8 us
  Pallas kernels  76.1 us (95%)
  local copies, waits for them, and re-layouts  2.91 us (4%)
    pallas_call x1, Pallas kernels, per_device(): pl.pallas_call(kernel, out_shape=jax.ShapeDtypeStruct((MB * 32, 256), f32...  76.1 us
    unnamed x10, local copies, waits for them, and re-layouts  2.91 us

profile of v1, /device:TPU:2, one launch (start us, length us, event | category | flops | bytes accessed | tf_op | source)
XLA Modules:
  0.0 79.8 jit_solution(10005431724153226046)
XLA Ops:
  0.7 0.0 copy-start
  0.7 0.0 copy-start.1
  0.7 0.0 copy-start.2
  0.7 0.0 copy-start.3
  0.7 1.9 %copy.9 = f32[32,1,1,8192]{3,0,1,2:T(8,128)S(1)} copy(f32[32,1,1,8192]{3,2,1,0:T(1,128)} %param.7) | data formatting | bytes 2097152
  2.6 0.0 copy-done
  2.6 0.0 copy-done.1
  2.6 0.0 copy-done.2
  2.6 0.0 copy-done.3
  2.7 76.1 %analysis.1 = f32[1024,256]{1,0:T(8,128)S(1)} custom-call(f32[1024,256]{1,0:T(8,128)S(1)} %bitcast.12, f32[32,8192]{1,0:T(8,128)S(1)} %bitcast.11, f32[1,1024]{1,0:T(1,128)S(1)} %bitcast.13, f32[1,1024]{1,0:T(1,128)S(1)} %bitcast.14, s32[1,1024]{1,0:T(1,128)S(1)} %bitcast.15, s32[1,1]{1,0:T(1,128)} %bitcast.9.tally), custom_call_target="tpu_custom_call" | custom-call | tf_op jit(solution)/shard_map/analysis/pallas_call | solution.py:396
  78.8 1.0 %copy.12 = f32[32,32,256]{2,1,0:T(8,128)} copy(f32[32,32,256]{2,1,0:T(8,128)S(1)} %bitcast.10) | data formatting | bytes 2097152
Async XLA Ops:
  0.7 2.0 %copy-start = (f32[32,32,256]{2,1,0:T(8,128)S(1)}, f32[32,32,256]{2,1,0:T(8,128)}, u32[]{:S(2)}) copy-start(f32[32,32,256]{2,1,0:T(8,128)} %param.6) | copy-start | bytes 3145732
  0.7 2.0 %copy-start.1 = (f32[1,1,1,1024]{3,2,1,0:T(1,128)S(1)}, f32[1,1,1,1024]{3,2,1,0:T(1,128)}, u32[]{:S(2)}) copy-start(f32[1,1,1,1024]{3,2,1,0:T(1,128)} %param.8) | copy-start | bytes 12292
  0.7 2.0 %copy-start.2 = (f32[1,1,1,1024]{3,2,1,0:T(1,128)S(1)}, f32[1,1,1,1024]{3,2,1,0:T(1,128)}, u32[]{:S(2)}) copy-start(f32[1,1,1,1024]{3,2,1,0:T(1,128)} %param.9) | copy-start | bytes 12292
  0.7 2.0 %copy-start.3 = (s32[1,1,1,1024]{3,2,1,0:T(1,128)S(1)}, s32[1,1,1,1024]{3,2,1,0:T(1,128)}, u32[]{:S(2)}) copy-start(s32[1,1,1,1024]{3,2,1,0:T(1,128)} %param.10) | copy-start | bytes 12292

commit v2 on v1

--- a/solution.py
+++ b/solution.py
@@ -7,7 +7,7 @@
 from jax.experimental.pallas import tpu as pltpu
 from jax.sharding import PartitionSpec as P
 
-NS_PASSES = (3, 3, 3, 3, 2, 2)
+Y_PARTS = (3, 3, 3, 3, 2, 2)
 MESH = pl.DeviceIdType.MESH
 f32 = jnp.float32
 bf16 = jnp.bfloat16
@@ -65,7 +65,7 @@
 def kernel(
     bg, obs, dep, var, anchor, tally,
     out,
-    bgs, outs, pk, yb, wts, cov, rhs, norm, y0, y1, y2, y3, z0, z1, z2, z3,
+    bgs, pk, yb, wts, cov, rhs, norm, y0, y1, y2, y3, z0, z1, z2, z3,
     pb, bh, bl, bh3, bl3, means, ts, tl, tr, cb, rb,
     bg_in, obs_send, obs_recv, bg_send, bg_recv, t_send, t_recv, c_send, c_recv,
 ):
@@ -166,42 +166,59 @@
         rhs[...] += product(split(wts[:, lanes], 3), yt)
         return carry
 
-    lax.fori_loop(0, CHUNKS - 1, cov_step, 0)
-
-    def bg_copies(b):
+    cov_step(jnp.int32(0), 0)
+
+    def bg_start(g):
         def copy(src, dst, where):
             return pltpu.make_async_remote_copy(
-                src_ref=src, dst_ref=dst, send_sem=bg_send, recv_sem=bg_recv,
+                src_ref=src, dst_ref=dst, send_sem=bg_send, recv_sem=bg_recv.at[g],
                 device_id=where, device_id_type=MESH,
             )
 
-        to_next = lax.rem(gy + jnp.where(b == 0, 1, 0), 4)
-        to_prev = lax.rem(gy + jnp.where(b == NB - 1, 3, 0), 4)
-        below, above = lax.rem(2 * b + 15, 16), lax.rem(2 * b + 2, 16)
-        return (
-            lambda: copy(pk.at[pl.ds(2 * b, 2)], pb.at[pl.ds(1, 2), :, mine, :], {"mem": b}),
-            lambda: copy(pk.at[below], pb.at[0, :, mine, :], {"mem": b, "gy": to_next}),
-            lambda: copy(pk.at[above], pb.at[3, :, mine, :], {"mem": b, "gy": to_prev}),
-        )
-
-    def start_bg(b):
-        for copy in bg_copies(b):
-            copy().start()
-
-    each_peer(start_bg)
-    pltpu.make_async_copy(pk.at[pl.ds(2 * me, 2)], pb.at[pl.ds(1, 2), :, mine, :], bg_recv).start()
-    for s, edge, which in ((0, 0, 1), (3, NB - 1, 2)):
-
-        @pl.when(me == edge)
-        def _():
-            bg_copies(me)[which]().start()
-
-        @pl.when(me != edge)
-        def _():
-            u = lax.rem(2 * me + (15 if s == 0 else 2), 16)
-            pltpu.make_async_copy(pk.at[u], pb.at[s, :, mine, :], bg_recv).start()
-
-    cov_step(jnp.int32(CHUNKS - 1), 0)
+        def inner_copy(b):
+            first = jnp.clip(2 * b - 1, 0, 12)
+            return pk.at[pl.ds(first, 4), g], pb.at[:, g, mine, :]
+
+        def middle_copy(b):
+            return pk.at[pl.ds(2 * b, 2), g], pb.at[pl.ds(1, 2), g, mine, :]
+
+        def side_copy(b, s):
+            u = lax.rem(2 * b + (15 if s == 0 else 2), 16)
+            return pk.at[u, g], pb.at[s, g, mine, :]
+
+        def side_start(b, s):
+            step = jnp.where(b == 0, 1, 0) if s == 0 else jnp.where(b == NB - 1, 3, 0)
+            copy(*side_copy(b, s), {"mem": b, "gy": lax.rem(gy + step, 4)}).start()
+
+        def start(b):
+            within = (b > 0) & (b < NB - 1)
+
+            @pl.when(within)
+            def _():
+                copy(*inner_copy(b), {"mem": b}).start()
+
+            @pl.when(jnp.logical_not(within))
+            def _():
+                copy(*middle_copy(b), {"mem": b}).start()
+                side_start(b, 0)
+                side_start(b, 3)
+
+        each_peer(start)
+        pltpu.make_async_copy(*middle_copy(me), bg_recv.at[g]).start()
+        for s, edge in ((0, 0), (3, NB - 1)):
+
+            @pl.when(me == edge)
+            def _():
+                side_start(me, s)
+
+            @pl.when(me != edge)
+            def _():
+                pltpu.make_async_copy(*side_copy(me, s), bg_recv.at[g]).start()
+
+    for g in range(4):
+        bg_start(g)
+
+    lax.fori_loop(1, CHUNKS, cov_step, 0)
 
     row_id = lax.broadcasted_iota(jnp.int32, (K, K), 0)
     eye = (row_id == lax.broadcasted_iota(jnp.int32, (K, K), 1)).astype(f32)
@@ -216,14 +233,14 @@
         return [2.25 * eye - 0.75 * x[p] - 0.5 * v[p] for p in points]
 
     def pair(n, last):
-        zp = [split(z[...], n) for z in zs]
+        zp = [split(z[...], 2) for z in zs]
         yp = [split(y[...], n) for y in ys]
-        w = two_steps([product(zp[p], yp[p]) for p in points], n)
+        w = two_steps([product(zp[p], yp[p][:2]) for p in points], 2)
         wp = [split(a, n) for a in w]
         for p in points:
             if not last:
                 ys[p][...] = product(yp[p], wp[p])
-            zs[p][...] = product(wp[p], zp[p])
+            zs[p][...] = product(wp[p][:2], zp[p])
 
     scaled = []
     for p in points:
@@ -231,14 +248,14 @@
         size = jnp.sqrt(jnp.sum(full * full, axis=(0, 1), keepdims=True))
         norm[p : p + 1, :] = jnp.broadcast_to(size, (1, LN))
         scaled.append(full * (1.0 / size))
-    w = two_steps(scaled, NS_PASSES[0])
+    w = two_steps(scaled, 2)
     for p in points:
-        ys[p][...] = product(split(scaled[p], NS_PASSES[0]), split(w[p], NS_PASSES[0]))
+        ys[p][...] = product(split(scaled[p], Y_PARTS[0]), split(w[p], Y_PARTS[0]))
         zs[p][...] = w[p]
-    exact = sum(1 for n in NS_PASSES[1:] if n == 3)
+    exact = sum(1 for n in Y_PARTS[1:] if n == 3)
     lax.fori_loop(0, exact, lambda i, carry: (pair(3, False), carry)[1], 0)
     for k in range(1 + exact, 6):
-        pair(NS_PASSES[k], k == 5)
+        pair(Y_PARTS[k], k == 5)
 
     def finish(p):
         z = zs[p][...]
@@ -260,26 +277,29 @@
     finish(3)
     to_right.start()
     finish(1)
-    finish(2)
-
-    pltpu.make_async_copy(pb, pb, bg_recv).wait()
+
     lane = lax.broadcasted_iota(jnp.int32, (1, LN), 1)
     xx = lane // 16
     weight_right = (xx.astype(f32) + 0.5) / 8.0
     weight_left = 1.0 - weight_right
     south_end = (me == 0) & (gy == 0)
     north_end = (me == NB - 1) & (gy == 3)
+    tents = []
     for s in range(4):
         tent = 1.0 - jnp.abs((lane % 16).astype(f32) + (16 * s + 0.5 - 32.0)) / 32.0
         end = south_end if s < 2 else north_end
-        tent = jnp.where(end, 0.0 if s in (0, 3) else 1.0, tent)
-        cols = slice(s * LN, (s + 1) * LN)
-        for g in range(4):
+        tents.append(jnp.where(end, 0.0 if s in (0, 3) else 1.0, tent))
+
+    def prepare(g):
+        here = pb.at[:, g]
+        pltpu.make_async_copy(here, here, bg_recv.at[g]).wait()
+        for s in range(4):
+            cols = slice(s * LN, (s + 1) * LN)
             slab = pb[s, g]
             mean = jnp.sum(slab, axis=0, keepdims=True) * (1.0 / K)
             means[4 * s + g : 4 * s + g + 1, :] = mean
             slab = slab - mean
-            left, right = slab * (tent * weight_left), slab * (tent * weight_right)
+            left, right = slab * (tents[s] * weight_left), slab * (tents[s] * weight_right)
             if g < 3:
                 for i, part in enumerate((left, right)):
                     hi, lo = split(part, 2)
@@ -314,10 +334,26 @@
             lambda: copy(cb.at[g, 3, rows, :], rb.at[g, odd, above], {"mem": j, "gy": gy_above}),
         )
 
+    inner = (me > 0) & (me < NB - 1)
+
+    def c_whole(g, j):
+        rows = pl.ds(pl.multiple_of(j * MB, MB), MB)
+        first = jnp.clip(2 * me - 1, 0, 12)
+        return pltpu.make_async_remote_copy(
+            src_ref=cb.at[g, :, rows, :], dst_ref=rb.at[g, odd, pl.ds(first, 4)],
+            send_sem=c_send, recv_sem=c_recv.at[g], device_id={"mem": j}, device_id_type=MESH,
+        )
+
     def start_c(g):
         def start(j):
-            for copy in c_copies(g, j):
-                copy().start()
+            @pl.when(inner)
+            def _():
+                c_whole(g, j).start()
+
+            @pl.when(jnp.logical_not(inner))
+            def _():
+                for copy in c_copies(g, j):
+                    copy().start()
 
         each_peer(start)
         pltpu.make_async_copy(
@@ -351,8 +387,12 @@
                 cb[g, s] = part
 
     for g in range(3):
+        if g == 1:
+            finish(2)
+        prepare(g)
         shares(g, [ts[g], ts[g + 1]], bh.at[g], bl.at[g])
         start_c(g)
+    prepare(3)
     to_left.wait_recv()
     to_right.wait_recv()
     shares(3, [ts[3], tr[...], tl[...], ts[0]], bh3, bl3)
@@ -363,13 +403,7 @@
         for half in range(2):
             v = [rb[g, 0, half * 8 + i] + rb[g, 1, half * 8 + i] for i in range(8)]
             for xx_, w in enumerate(block_transpose(v)):
-                outs[half, pl.ds(column_of(g, xx_), MB, stride=32), :] = w
-    stores = [pltpu.make_async_copy(outs.at[h], out.at[:, halves[h]], bg_in.at[h]) for h in range(2)]
-    for store in stores:
-        store.start()
-
-    for store in stores:
-        store.wait()
+                out[half, pl.ds(column_of(g, xx_), MB, stride=32), :] = w
 
     to_left.wait_send()
     to_right.wait_send()
@@ -395,11 +429,10 @@
     dma = pltpu.SemaphoreType.DMA
     out = pl.pallas_call(
         kernel,
-        out_shape=jax.ShapeDtypeStruct((MB * 32, 256), f32),
+        out_shape=jax.ShapeDtypeStruct((2, MB * 32, LN), f32),
         in_specs=[anywhere, anywhere, vmem, vmem, vmem, vmem],
-        out_specs=anywhere,
+        out_specs=vmem,
         scratch_shapes=[
-            pltpu.VMEM((2, MB * 32, LN), f32),
             pltpu.VMEM((2, MB * 32, LN), f32),
             pltpu.VMEM((16, 4, MB, LN), f32),
             pltpu.VMEM((K, SLOTS), f32),
@@ -423,7 +456,7 @@
             dma,
             dma((CHUNKS,)),
             dma,
-            dma,
+            dma((4,)),
             dma((2,)),
             dma((2,)),
             dma,
@@ -441,7 +474,7 @@
         anchor.reshape(1, SLOTS),
         tally.reshape(1, 1),
     )
-    return out.reshape(MB, 32, 256)
+    return out.reshape(2, MB, 32, LN).transpose(1, 2, 0, 3).reshape(MB, 32, 256)
 
 
 def solution(mesh):

time: 80.3 us -> 76.9 us (0.958)
  Pallas kernels: 76.1 us -> 73.1 us
    pallas_call x1, Pallas kernels: 76.1 us -> 73.1 us  [per_device(): pl.pallas_call(kernel, out_shape=jax.ShapeDtypeStruct((2, MB * 32, LN), f...]
    reshape x0 -> x1, local copies, waits for them, and re-layouts: none -> 1.06 us  [per_device(): return out.reshape(2, MB, 32, LN).transpose(1, 2, 0, 3).reshape(MB, 32, 256)]
    unnamed x10 -> x9, local copies, waits for them, and re-layouts: 2.91 us -> 1.93 us
where the time goes in v2:
time: 76.9 us; the launch traced here: 76.8 us
  Pallas kernels  73.1 us (95%)
  local copies, waits for them, and re-layouts  2.99 us (4%)
    pallas_call x1, Pallas kernels, per_device(): pl.pallas_call(kernel, out_shape=jax.ShapeDtypeStruct((2, MB * 32, LN), f...  73.1 us
    unnamed x9, local copies, waits for them, and re-layouts  1.93 us

profile of v2, /device:TPU:2, one launch (start us, length us, event | category | flops | bytes accessed | tf_op | source)
XLA Modules:
  0.0 76.8 jit_solution(10743331996740990894)
XLA Ops:
  0.7 0.0 copy-start
  0.7 0.0 copy-start.1
  0.7 0.0 copy-start.2
  0.7 0.0 copy-start.3
  0.7 1.9 %copy.13 = f32[32,1,1,8192]{3,0,1,2:T(8,128)S(1)} copy(f32[32,1,1,8192]{3,2,1,0:T(1,128)} %param.7) | data formatting | bytes 2097152
  2.6 0.0 copy-done
  2.6 0.0 copy-done.1
  2.6 0.0 copy-done.2
  2.6 0.0 copy-done.3
  2.7 73.1 %analysis.1 = f32[2,1024,128]{2,1,0:T(8,128)S(1)} custom-call(f32[1024,256]{1,0:T(8,128)S(1)} %bitcast.18, f32[32,8192]{1,0:T(8,128)S(1)} %bitcast.17, f32[1,1024]{1,0:T(1,128)S(1)} %bitcast.19, f32[1,1024]{1,0:T(1,128)S(1)} %bitcast.20, s32[1,1024]{1,0:T(1,128)S(1)} %bitcast.21, s32[1,1]{1,0:T(1,128)} %bitcast.15.tally), custom_call_target="tpu_custom_call" | custom-call | tf_op jit(solution)/shard_map/analysis/pallas_call | solution.py:430
  75.7 1.1 %copy.12 = f32[2,32,4,8,128]{4,3,0,2,1:T(8,128)} copy(f32[2,32,4,8,128]{4,3,2,1,0:T(8,128)S(1)} %bitcast.16) | data formatting | bytes 2097152 | tf_op jit(solution)/shard_map/reshape | solution.py:477
Async XLA Ops:
  0.7 2.0 %copy-start = (f32[32,32,256]{2,1,0:T(8,128)S(1)}, f32[32,32,256]{2,1,0:T(8,128)}, u32[]{:S(2)}) copy-start(f32[32,32,256]{2,1,0:T(8,128)} %param.6) | copy-start | bytes 3145732
  0.7 2.0 %copy-start.1 = (f32[1,1,1,1024]{3,2,1,0:T(1,128)S(1)}, f32[1,1,1,1024]{3,2,1,0:T(1,128)}, u32[]{:S(2)}) copy-start(f32[1,1,1,1024]{3,2,1,0:T(1,128)} %param.8) | copy-start | bytes 12292
  0.7 2.0 %copy-start.2 = (f32[1,1,1,1024]{3,2,1,0:T(1,128)S(1)}, f32[1,1,1,1024]{3,2,1,0:T(1,128)}, u32[]{:S(2)}) copy-start(f32[1,1,1,1024]{3,2,1,0:T(1,128)} %param.9) | copy-start | bytes 12292
  0.7 2.0 %copy-start.3 = (s32[1,1,1,1024]{3,2,1,0:T(1,128)S(1)}, s32[1,1,1,1024]{3,2,1,0:T(1,128)}, u32[]{:S(2)}) copy-start(s32[1,1,1,1024]{3,2,1,0:T(1,128)} %param.10) | copy-start | bytes 12292

commit v3 on v2

--- a/solution.py
+++ b/solution.py
@@ -94,26 +94,11 @@
 
         lax.fori_loop(1, NB, step, 0)
 
-    def each_member(fn):
-        def step(j, carry):
-            fn(j)
-            return carry
-
-        lax.fori_loop(0, NB, step, 0)
-
     each_peer(lambda j: greet(mem=j))
     greet(gx=gx_left)
     greet(gx=gx_right)
-    greet(mem=jnp.int32(0), gy=gy_next)
-    greet(mem=jnp.int32(NB - 1), gy=gy_prev)
-
-    @pl.when(me == 0)
-    def _():
-        each_member(lambda j: greet(mem=j, gy=gy_prev))
-
-    @pl.when(me == NB - 1)
-    def _():
-        each_member(lambda j: greet(mem=j, gy=gy_next))
+    greet(gy=gy_prev)
+    greet(gy=gy_next)
 
     mine = pl.ds(pl.multiple_of(me * MB, MB), MB)
 
@@ -124,7 +109,7 @@
         wts[p : p + 1, :] = weight
         wts[p + 4 : p + 5, :] = weight * dep[...]
 
-    pl.semaphore_wait(barrier, 11 + jnp.where((me == 0) | (me == NB - 1), NB, 0))
+    pl.semaphore_wait(barrier, NB + 3)
 
     def obs_copy(c, j):
         first = pl.multiple_of(j * SLOTS + c * CW, CW)

time: 76.9 us -> 74.6 us (0.970)
  Pallas kernels: 73.1 us -> 70.6 us
    pallas_call x1, Pallas kernels: 73.1 us -> 70.6 us  [per_device(): pl.pallas_call(kernel, out_shape=jax.ShapeDtypeStruct((2, MB * 32, LN), f...]
where the time goes in v3:
time: 74.6 us; the launch traced here: 74.3 us
  Pallas kernels  70.6 us (95%)
  local copies, waits for them, and re-layouts  2.99 us (4%)
    pallas_call x1, Pallas kernels, per_device(): pl.pallas_call(kernel, out_shape=jax.ShapeDtypeStruct((2, MB * 32, LN), f...  70.6 us
    unnamed x9, local copies, waits for them, and re-layouts  1.93 us

profile of v3, /device:TPU:2, one launch (start us, length us, event | category | flops | bytes accessed | tf_op | source)
XLA Modules:
  0.0 74.3 jit_solution(2358254840490366340)
XLA Ops:
  0.7 0.0 copy-start
  0.7 0.0 copy-start.1
  0.7 0.0 copy-start.2
  0.7 0.0 copy-start.3
  0.7 1.9 %copy.13 = f32[32,1,1,8192]{3,0,1,2:T(8,128)S(1)} copy(f32[32,1,1,8192]{3,2,1,0:T(1,128)} %param.7) | data formatting | bytes 2097152
  2.6 0.0 copy-done
  2.6 0.0 copy-done.1
  2.6 0.0 copy-done.2
  2.6 0.0 copy-done.3
  2.7 70.6 %analysis.1 = f32[2,1024,128]{2,1,0:T(8,128)S(1)} custom-call(f32[1024,256]{1,0:T(8,128)S(1)} %bitcast.18, f32[32,8192]{1,0:T(8,128)S(1)} %bitcast.17, f32[1,1024]{1,0:T(1,128)S(1)} %bitcast.19, f32[1,1024]{1,0:T(1,128)S(1)} %bitcast.20, s32[1,1024]{1,0:T(1,128)S(1)} %bitcast.21, s32[1,1]{1,0:T(1,128)} %bitcast.15.tally), custom_call_target="tpu_custom_call" | custom-call | tf_op jit(solution)/shard_map/analysis/pallas_call | solution.py:415
  73.3 1.1 %copy.12 = f32[2,32,4,8,128]{4,3,0,2,1:T(8,128)} copy(f32[2,32,4,8,128]{4,3,2,1,0:T(8,128)S(1)} %bitcast.16) | data formatting | bytes 2097152 | tf_op jit(solution)/shard_map/reshape | solution.py:462
Async XLA Ops:
  0.7 2.0 %copy-start = (f32[32,32,256]{2,1,0:T(8,128)S(1)}, f32[32,32,256]{2,1,0:T(8,128)}, u32[]{:S(2)}) copy-start(f32[32,32,256]{2,1,0:T(8,128)} %param.6) | copy-start | bytes 3145732
  0.7 2.0 %copy-start.1 = (f32[1,1,1,1024]{3,2,1,0:T(1,128)S(1)}, f32[1,1,1,1024]{3,2,1,0:T(1,128)}, u32[]{:S(2)}) copy-start(f32[1,1,1,1024]{3,2,1,0:T(1,128)} %param.8) | copy-start | bytes 12292
  0.7 2.0 %copy-start.2 = (f32[1,1,1,1024]{3,2,1,0:T(1,128)S(1)}, f32[1,1,1,1024]{3,2,1,0:T(1,128)}, u32[]{:S(2)}) copy-start(f32[1,1,1,1024]{3,2,1,0:T(1,128)} %param.9) | copy-start | bytes 12292
  0.7 2.0 %copy-start.3 = (s32[1,1,1,1024]{3,2,1,0:T(1,128)S(1)}, s32[1,1,1,1024]{3,2,1,0:T(1,128)}, u32[]{:S(2)}) copy-start(s32[1,1,1,1024]{3,2,1,0:T(1,128)} %param.10) | copy-start | bytes 12292

commit v4 on v3

--- a/solution.py
+++ b/solution.py
@@ -79,9 +79,6 @@
 
     halves = [slice(0, LN), slice(LN, 2 * LN)]
     loads = [pltpu.make_async_copy(bg.at[:, halves[h]], bgs.at[h], bg_in.at[h]) for h in range(2)]
-    for load in loads:
-        load.start()
-
     barrier = pltpu.get_barrier_semaphore()
 
     def greet(**where):
@@ -94,11 +91,14 @@
 
         lax.fori_loop(1, NB, step, 0)
 
-    each_peer(lambda j: greet(mem=j))
+    greet(gy=gy_prev)
+    greet(gy=gy_next)
     greet(gx=gx_left)
     greet(gx=gx_right)
-    greet(gy=gy_prev)
-    greet(gy=gy_next)
+    each_peer(lambda j: greet(mem=j))
+
+    for load in loads:
+        load.start()
 
     mine = pl.ds(pl.multiple_of(me * MB, MB), MB)
 

time: 74.6 us -> 74.4 us (level)
  no operation moved by 1% of the time
where the time goes in v4:
time: 74.4 us; the launch traced here: 74.1 us
  Pallas kernels  70.4 us (95%)
  local copies, waits for them, and re-layouts  2.99 us (4%)
    pallas_call x1, Pallas kernels, per_device(): pl.pallas_call(kernel, out_shape=jax.ShapeDtypeStruct((2, MB * 32, LN), f...  70.4 us
    unnamed x9, local copies, waits for them, and re-layouts  1.93 us

profile of v4, /device:TPU:2, one launch (start us, length us, event | category | flops | bytes accessed | tf_op | source)
XLA Modules:
  0.0 74.1 jit_solution(863427575143810583)
XLA Ops:
  0.7 0.0 copy-start
  0.7 0.0 copy-start.1
  0.7 0.0 copy-start.2
  0.7 0.0 copy-start.3
  0.7 1.9 %copy.13 = f32[32,1,1,8192]{3,0,1,2:T(8,128)S(1)} copy(f32[32,1,1,8192]{3,2,1,0:T(1,128)} %param.7) | data formatting | bytes 2097152
  2.6 0.0 copy-done
  2.6 0.0 copy-done.1
  2.6 0.0 copy-done.2
  2.6 0.0 copy-done.3
  2.7 70.4 %analysis.1 = f32[2,1024,128]{2,1,0:T(8,128)S(1)} custom-call(f32[1024,256]{1,0:T(8,128)S(1)} %bitcast.18, f32[32,8192]{1,0:T(8,128)S(1)} %bitcast.17, f32[1,1024]{1,0:T(1,128)S(1)} %bitcast.19, f32[1,1024]{1,0:T(1,128)S(1)} %bitcast.20, s32[1,1024]{1,0:T(1,128)S(1)} %bitcast.21, s32[1,1]{1,0:T(1,128)} %bitcast.15.tally), custom_call_target="tpu_custom_call" | custom-call | tf_op jit(solution)/shard_map/analysis/pallas_call | solution.py:415
  73.1 1.1 %copy.12 = f32[2,32,4,8,128]{4,3,0,2,1:T(8,128)} copy(f32[2,32,4,8,128]{4,3,2,1,0:T(8,128)S(1)} %bitcast.16) | data formatting | bytes 2097152 | tf_op jit(solution)/shard_map/reshape | solution.py:462
Async XLA Ops:
  0.7 2.0 %copy-start = (f32[32,32,256]{2,1,0:T(8,128)S(1)}, f32[32,32,256]{2,1,0:T(8,128)}, u32[]{:S(2)}) copy-start(f32[32,32,256]{2,1,0:T(8,128)} %param.6) | copy-start | bytes 3145732
  0.7 2.0 %copy-start.1 = (f32[1,1,1,1024]{3,2,1,0:T(1,128)S(1)}, f32[1,1,1,1024]{3,2,1,0:T(1,128)}, u32[]{:S(2)}) copy-start(f32[1,1,1,1024]{3,2,1,0:T(1,128)} %param.8) | copy-start | bytes 12292
  0.7 2.0 %copy-start.2 = (f32[1,1,1,1024]{3,2,1,0:T(1,128)S(1)}, f32[1,1,1,1024]{3,2,1,0:T(1,128)}, u32[]{:S(2)}) copy-start(f32[1,1,1,1024]{3,2,1,0:T(1,128)} %param.9) | copy-start | bytes 12292
  0.7 2.0 %copy-start.3 = (s32[1,1,1,1024]{3,2,1,0:T(1,128)S(1)}, s32[1,1,1,1024]{3,2,1,0:T(1,128)}, u32[]{:S(2)}) copy-start(s32[1,1,1,1024]{3,2,1,0:T(1,128)} %param.10) | copy-start | bytes 12292
